TPU v7x, 32 devices: a whole 2x2x4 slice. The times are simulated.
32 devices in a mesh: section: 8 (over z, y), expert: 4 (over x, core).
Axes of the slice: x: 2, y: 2, z: 4, core: 2. Of those that a mesh axis runs over, the one named last changes fastest.
Arguments:
- carried: bfloat16 [8, 512, 2048], P('section', 'expert'), may hold values from -6 to 6
- halting: int32 [8, 512], P('section', 'expert'), may hold values from 1 to 2
- section_lap: int32 [8], P('section'), may hold values from 1 to 2
- routing: int32 [8, 512, 8], P('section', 'expert'), may hold values from 0 to 63, all different within a row; in each aligned block of 128 rows (0 to 127, 128 to 255, ..., all dimensions but the last counted through in order) at most 24 rows name the same one
- attention_gain: float32 [8, 2048], P('section'), may hold values from 0.25 to 1.75
- attention_in: bfloat16 [8, 2048, 3, 2048], P('section', None, None, 'expert')
- attention_out: bfloat16 [8, 2048, 2048], P('section', 'expert'), may hold values from -0.125 to 0.125
- expert_gain: float32 [8, 2048], P('section'), may hold values from 0.25 to 1.75
- router: bfloat16 [8, 2048, 64], P('section'), may hold values from -0.125 to 0.125
- expert_in: bfloat16 [8, 64, 2048, 256], P('section', 'expert'), may hold values from -0.125 to 0.125
- expert_out: bfloat16 [8, 64, 256, 2048], P('section', 'expert'), may hold values from -0.375 to 0.375
Outputs:
- stepped: bfloat16 [8, 512, 2048], P('section', 'expert')
Inputs may be any that keep to these rules, and one draw needn't show every extreme that they name: `routing`: within each aligned block of 128 consecutive tokens of a section's micro-batch, no expert is named by more than 24 tokens, and the 8 experts of one token differ.
All inputs are finite; a program needn't handle non-finite values.
Results may differ from a plain program's by a relative error of at most 0.013.
The roundings to bfloat16 on the way count: a program that leaves them out, or rounds other values in their place, can miss the bound.
Values may be sent and summed in bfloat16 or wider, within the bound.
A program may use at most 192 MiB of HBM per device.

v0:
```python
import jax
import jax.numpy as jnp
from jax import lax
from jax.sharding import PartitionSpec as P

TOPK = 8
HEAD_SIZE = 128
CAP = 24


EPSILON = 1e-06


def passed_along(block, axis, distance):
    devices = range(lax.axis_size(axis))
    route = [((i - distance) % len(devices), i) for i in devices]
    return lax.ppermute(block, axis, route)


def rms_scale(inputs, gain_row):
    mean_sq = jnp.mean(inputs * inputs, axis=-1, keepdims=True)
    return inputs * lax.rsqrt(mean_sq + EPSILON) * gain_row


def block_positions(routes, active, experts_total):
    expert_ids = jnp.arange(experts_total, dtype=jnp.int32)
    one_hot = (routes[:, :, None] == expert_ids).astype(jnp.int32) * active[:, None, None].astype(
        jnp.int32
    )
    flat_hot = one_hot.reshape(-1, experts_total)
    before = jnp.cumsum(flat_hot, axis=0) - flat_hot
    return jnp.sum(before * flat_hot, axis=1).reshape(routes.shape)


def local(
    carried,
    halting,
    section_lap,
    routing,
    attention_gain,
    attention_in,
    attention_out,
    expert_gain,
    router,
    expert_in,
    expert_out,
):
    incoming = passed_along(carried, "section", 1)[0]
    tok_dev = incoming.shape[0]
    model_width = incoming.shape[1]
    groups = lax.axis_size("expert")
    residual = incoming.astype(jnp.float32)
    normed = rms_scale(residual, attention_gain[0]).astype(jnp.bfloat16)
    qkv_cols = attention_in[0].reshape(model_width, -1)
    head_cols = qkv_cols.shape[1] // 3
    heads_here = head_cols // HEAD_SIZE
    projected = jnp.dot(
        lax.all_gather(normed, "expert", axis=0, tiled=True),
        qkv_cols,
        preferred_element_type=jnp.float32,
    ).astype(jnp.bfloat16)
    seq_len = projected.shape[0]
    queries = projected[:, :head_cols].reshape(seq_len, heads_here, HEAD_SIZE)
    keys_all = projected[:, head_cols : 2 * head_cols].reshape(seq_len, heads_here, HEAD_SIZE)
    values_all = projected[:, 2 * head_cols :].reshape(seq_len, heads_here, HEAD_SIZE)
    row_block = min(512, seq_len)

    def attend_block(block_index):
        first_row = block_index * row_block
        query_rows = lax.dynamic_slice_in_dim(queries, first_row, row_block, 0)
        scores = jnp.einsum(
            "qhc,khc->hqk", query_rows, keys_all, preferred_element_type=jnp.float32
        ) * HEAD_SIZE ** (-0.5)
        row_ids = first_row + lax.broadcasted_iota(jnp.int32, (1, row_block, seq_len), 1)
        col_ids = lax.broadcasted_iota(jnp.int32, (1, row_block, seq_len), 2)
        scores = jnp.where(col_ids <= row_ids, scores, -jnp.inf)
        row_max = jnp.max(scores, axis=-1, keepdims=True)
        weights = jnp.exp(scores - row_max)
        weights = (weights / jnp.sum(weights, axis=-1, keepdims=True)).astype(jnp.bfloat16)
        return jnp.einsum(
            "hqk,khc->qhc", weights, values_all, preferred_element_type=jnp.float32
        ).astype(jnp.bfloat16)

    attended = lax.map(attend_block, jnp.arange(seq_len // row_block, dtype=jnp.int32)).reshape(
        seq_len, head_cols
    )
    out_rows = attention_out[0]
    attention_sum = lax.psum_scatter(
        jnp.dot(attended, out_rows, preferred_element_type=jnp.float32).astype(jnp.bfloat16),
        "expert",
        scatter_dimension=0,
        tiled=True,
    ).astype(jnp.float32)
    updated = residual + attention_sum
    expert_input = rms_scale(updated, expert_gain[0]).astype(jnp.bfloat16)
    active = halting[0] >= section_lap[0]
    routes = routing[0]
    experts_total = router.shape[2]
    exp_local = expert_in.shape[1]
    gate_all = jax.nn.sigmoid(jnp.dot(expert_input, router[0], preferred_element_type=jnp.float32))
    expert_ids = jnp.arange(experts_total, dtype=jnp.int32)
    gate_vals = jnp.sum(
        jnp.where(routes[:, :, None] == expert_ids, gate_all[:, None, :], 0.0), axis=2
    )
    slot_pos = block_positions(routes, active, experts_total)
    slot_index = jnp.where(active[:, None], routes * CAP + slot_pos, experts_total * CAP)
    copies = jnp.broadcast_to(expert_input[:, None, :], (tok_dev, TOPK, model_width)).reshape(
        -1, model_width
    )
    outgoing = (
        jnp.zeros((experts_total * CAP, model_width), jnp.bfloat16)
        .at[slot_index.reshape(-1)]
        .set(copies, mode="drop")
    )
    arrived = lax.all_to_all(
        outgoing.reshape(groups, -1, model_width), "expert", split_axis=0, concat_axis=0, tiled=True
    )
    arrived = arrived.reshape(groups, exp_local, CAP, model_width)
    hidden = jax.nn.relu(
        jnp.einsum("secd,edh->sech", arrived, expert_in[0], preferred_element_type=jnp.float32)
    ).astype(jnp.bfloat16)
    produced = jnp.einsum(
        "sech,ehd->secd", hidden, expert_out[0], preferred_element_type=jnp.float32
    ).astype(jnp.bfloat16)
    returned = lax.all_to_all(
        produced.reshape(groups, -1, model_width), "expert", split_axis=0, concat_axis=0, tiled=True
    )
    returned = returned.reshape(-1, model_width)
    picked = returned[jnp.where(active[:, None], slot_index, 0)]
    weight = jnp.where(active[:, None], gate_vals, 0.0)
    expert_sum = jnp.einsum("tk,tkd->td", weight, picked.astype(jnp.float32))
    stepped = jnp.where(active[:, None], updated + expert_sum, residual).astype(jnp.bfloat16)
    return stepped[None]


def solution(mesh):
    in_specs = (
        P("section", "expert", None),
        P("section", "expert"),
        P("section"),
        P("section", "expert", None),
        P("section", None),
        P("section", None, None, "expert"),
        P("section", "expert", None),
        P("section", None),
        P("section", None, None),
        P("section", "expert", None, None),
        P("section", "expert", None, None),
    )
    out_specs = P("section", "expert", None)
    return jax.shard_map(local, mesh=mesh, in_specs=in_specs, out_specs=out_specs, check_vma=False)
```

profile of v0, /device:TPU:0, one launch (start us, length us, event | category | flops | bytes accessed | tf_op | source)
XLA Modules:
  0.0 311.9 jit_solution(18055261769381287993)
XLA Ops:
  6.5 3.0 collective-permute-start
  9.5 15.2 %collective-permute-done = bf16[1,128,2048]{2,1,0:T(8,128)(2,1)S(1)} collective-permute-done((bf16[1,128,2048]{2,1,0:T(8,128)(2,1)}, bf16[1,128,2048]{2,1,0:T(8,128)(2,1)S(1)}, u32[]{:S(2)}, u32[]{:S(2)}) %collective-permute-start) | collective-permute-done | bytes 524320 | tf_op jit(solution)/shard_map/ppermute | solution.py:17
  24.7 0.2 fusion.37
  24.9 1.7 fusion.39
  26.6 8.9 %copy.41 = bf16[1,2048,3,512]{1,3,2,0:T(8,128)(2,1)} copy(bf16[1,2048,3,512]{3,1,2,0:T(8,128)(2,1)} %param.16) | data formatting | bytes 12582912 | tf_op args[5]
  35.5 0.1 iota_compare_fusion
  35.6 12.2 %all-gather.2.cloned.1.call-done = bf16[512,2048]{1,0:T(8,128)(2,1)} async-done(((bf16[128,2048]{1,0:T(8,128)(2,1)}), bf16[512,2048]{1,0:T(8,128)(2,1)}) %all-gather.2.cloned.1.call-update) | async-done | bytes 2097168 | tf_op jit(solution)/shard_map/all_gather | solution.py:58
  47.8 6.9 %convolution_convert_fusion.1 = bf16[512,1536]{1,0:T(8,128)(2,1)S(1)} fusion(bf16[512,2048]{1,0:T(8,128)(2,1)} %all-gather.2.cloned.1.call-done, bf16[2048,1536]{0,1:T(8,128)(2,1)} %bitcast.115), kind=kOutput, calls=%fused_computation.19 | convolution fusion | flops 3222011904 | bytes 9961472 | tf_op jit(solution)/shard_map/dot_general | solution.py:57
  54.6 1.2 slice_bitcast_fusion.1
  55.8 2.1 copy.59
  57.9 1.7 fusion.43
  59.6 2.1 fusion.58
  61.8 0.5 fusion.24
  62.3 2.6 convolution_convert_fusion
  65.0 0.1 copy.47
  65.1 0.1 eq.49
  65.2 0.1 eq.45
  65.9 0.1 reshape.242
  66.0 0.1 broadcast_in_dim.105.clone
  66.1 0.1 broadcast_in_dim.110
  66.2 0.1 mul.114
  66.3 0.1 mul.115
  66.4 0.1 mul.118
  66.5 0.1 mul.119
  66.6 0.1 mul.113
  66.7 18.0 %reduce-window.6 = s32[64,8,128]{2,1,0:T(8,128)S(1)} reduce-window(s32[64,8,128]{2,1,0:T(8,128)S(1)} %fusion.50, s32[]{:T(128)} %constant.48.clone.1), window={size=1x1x128 pad=0_0x0_0x127_0}, to_apply=%region_6.7 | reduce-window | flops 8323072 | bytes 524292 | tf_op jit(solution)/shard_map/reduce-window
  84.7 0.1 slice.25
  84.9 0.1 copy.49
  85.0 0.1 copy.50
  85.1 0.1 broadcast_add_fusion
  85.3 0.1 fusion.48
  85.4 11.3 %reduce-scatter.2.cloned.1.call-done = bf16[128,2048]{1,0:T(8,128)(2,1)} async-done(((bf16[512,2048]{1,0:T(8,128)(2,1)}), bf16[128,2048]{1,0:T(8,128)(2,1)}) %reduce-scatter.2.cloned.1.call-update) | async-done | bytes 524304 | tf_op jit(solution)/shard_map/reduce_scatter | solution.py:88
  96.7 1.3 multiply_reduce_fusion
  98.0 1.3 multiply_convert_fusion
  99.3 10.4 %scatter_custom_fusion = bf16[1536,2048]{1,0:T(8,128)(2,1)} fusion(s32[1024]{0:T(1024)S(1)} %bitcast.123, bf16[]{:T(256)} %constant.31.clone.1, bf16[128,2048]{1,0:T(8,128)(2,1)S(1)} %multiply_convert_fusion), kind=kCustom, calls=%fused_computation.11 | custom fusion | bytes 6815746 | tf_op jit(solution)/shard_map/scatter | solution.py:113
  109.7 77.4 %all_to_all.10 = bf16[4,384,2048]{2,1,0:T(8,128)(2,1)} all-to-all(bf16[4,384,2048]{2,1,0:T(8,128)(2,1)} %bitcast.114), channel_id=1, replica_groups=mesh['section'=8,'expert'=4] {'expert'}, dimensions={0} | all-to-all | bytes 12582912 | tf_op jit(solution)/shard_map/all_to_all | solution.py:115
  187.0 18.0 %convert_bitcast_fusion = bf16[4,16,24,2048]{3,2,0,1:T(8,128)(2,1)} fusion(bf16[1,16,256,2048]{3,2,1,0:T(8,128)(2,1)} %param.21, bf16[1,16,2048,256]{3,2,1,0:T(8,128)(2,1)} %param.20, bf16[4,16,24,2048]{3,2,1,0:T(8,128)(2,1)} %bitcast.112), kind=kOutput, calls=%fused_computation.8 | convolution fusion | flops 3225157632 | bytes 46137344 | tf_op jit(solution)/shard_map/sech,ehd->secd/dot_general | solution.py:122
  205.0 6.5 %copy.53 = bf16[4,16,24,2048]{3,2,1,0:T(8,128)(2,1)} copy(bf16[4,16,24,2048]{3,2,0,1:T(8,128)(2,1)} %convert_bitcast_fusion) | data formatting | bytes 12582912 | tf_op jit(solution)/shard_map/convert_element_type | solution.py:124
  211.5 5.4 %all-to-all-start.1 = ((bf16[4,384,2048]{2,1,0:T(8,128)(2,1)}), bf16[4,384,2048]{2,1,0:T(8,128)(2,1)}, u32[]{:S(2)}, u32[]{:S(2)}) async-start(bf16[4,384,2048]{2,1,0:T(8,128)(2,1)} %bitcast.113), calls=%async_computation.2 | async-start | bytes 12582912 | tf_op jit(solution)/shard_map/all_to_all | solution.py:125
  216.9 0.1 reshape.240
  217.0 0.1 compare_select_fusion
  217.1 0.1 reshape.245
  217.2 0.3 fusion.36
  217.6 0.1 copy.57
  217.7 69.9 %all-to-all-done.1 = bf16[4,384,2048]{2,1,0:T(8,128)(2,1)} async-done(((bf16[4,384,2048]{2,1,0:T(8,128)(2,1)}), bf16[4,384,2048]{2,1,0:T(8,128)(2,1)}, u32[]{:S(2)}, u32[]{:S(2)}) %all-to-all-start.1) | async-done | bytes 6291488 | tf_op jit(solution)/shard_map/all_to_all | solution.py:125
  287.6 12.6 %gather_fusion = bf16[1024,2048]{1,0:T(8,128)(2,1)} fusion(bf16[1536,2048]{1,0:T(8,128)(2,1)} %bitcast.30, s32[1024]{0:T(1024)S(1)} %broadcast_clamp_fusion), kind=kCustom, calls=%fused_computation | custom fusion | bytes 8392704 | tf_op jit(solution)/shard_map/gather | solution.py:129
  300.2 3.5 %fusion.8 = f32[128,1,2048]{2,1,0:T(1,128)S(1)} fusion(bf16[128,8,1]{1,2,0:T(2,128)(2,1)S(1)} %copy.57, bf16[1024,2048]{1,0:T(8,128)(2,1)} %gather_fusion), kind=kOutput, calls=%fused_computation.9 | convolution fusion | flops 4194304 | bytes 5244928 | tf_op jit(solution)/shard_map/tk,tkd->td/dot_general | solution.py:131
  303.7 1.4 fusion.42
  (32 shorter events, 0.3 us)
Async XLA Ops:
  6.5 55.7 %copy-start = (bf16[1,512,2048]{2,1,0:T(8,128)(2,1)S(1)}, bf16[1,512,2048]{2,1,0:T(8,128)(2,1)}, u32[]{:S(2)}) copy-start(bf16[1,512,2048]{2,1,0:T(8,128)(2,1)} %param.17) | copy-start | bytes 6291460
  6.5 41.2 %all-gather.2.cloned.1.call-start = ((), (), s32[]{:S(2)}) async-start(), calls=%async_computation.3 | async-start | bytes 2621440 | tf_op jit(solution)/shard_map/all_gather | solution.py:58
  6.5 18.1 %collective-permute-start = (bf16[1,128,2048]{2,1,0:T(8,128)(2,1)}, bf16[1,128,2048]{2,1,0:T(8,128)(2,1)S(1)}, u32[]{:S(2)}, u32[]{:S(2)}) collective-permute-start(bf16[1,128,2048]{2,1,0:T(8,128)(2,1)} %param.11), channel_id=1, source_target_pairs={{28,0},{0,4},{4,8},{8,12},{12,16},{16,20},{20,24},{24,28},{29,1},{... | collective-permute-start | bytes 1572872 | tf_op jit(solution)/shard_map/ppermute | solution.py:17
  26.6 70.1 %reduce-scatter.2.cloned.1.call-start = ((), (), s32[]{:S(2)}) async-start(), calls=%async_computation.4 | async-start | bytes 2621440 | tf_op jit(solution)/shard_map/reduce_scatter | solution.py:88
  59.6 2.2 copy-start.3
  62.3 2.7 copy-start.5
  62.3 3.6 %copy-start.7 = (s32[1,128]{1,0:T(1,128)S(1)}, s32[1,128]{1,0:T(1,128)}, u32[]{:S(2)}) copy-start(s32[1,128]{1,0:T(1,128)} %param.12) | copy-start | bytes 1540
  64.9 33.1 %copy-start.6 = (f32[1,2048]{1,0:T(1,128)S(1)}, f32[1,2048]{1,0:T(1,128)}, u32[]{:S(2)}) copy-start(f32[1,2048]{1,0:T(1,128)} %param.18) | copy-start | bytes 24580
  211.5 5.7 %copy-start.4 = (bf16[1,2048,64]{1,2,0:T(8,128)(2,1)S(1)}, bf16[1,2048,64]{1,2,0:T(8,128)(2,1)}, u32[]{:S(2)}) copy-start(bf16[1,2048,64]{1,2,0:T(8,128)(2,1)} %param.19) | copy-start | bytes 786436
  211.5 76.1 %all-to-all-start.1 = ((bf16[4,384,2048]{2,1,0:T(8,128)(2,1)}), bf16[4,384,2048]{2,1,0:T(8,128)(2,1)}, u32[]{:S(2)}, u32[]{:S(2)}) async-start(bf16[4,384,2048]{2,1,0:T(8,128)(2,1)} %bitcast.113), calls=%async_computation.2 | async-start | bytes 12582912 | tf_op jit(solution)/shard_map/all_to_all | solution.py:125
  287.6 17.4 %copy-start.1 = (bf16[1,512,2048]{2,1,0:T(8,128)(2,1)S(1)}, bf16[1,512,2048]{2,1,0:T(8,128)(2,1)}, u32[]{:S(2)}) copy-start(bf16[1,512,2048]{2,1,0:T(8,128)(2,1)} %param.17) | copy-start | bytes 6291460
  300.2 3.5 %copy-start.2 = (bf16[128,2048]{1,0:T(8,128)(2,1)S(1)}, bf16[128,2048]{1,0:T(8,128)(2,1)}, u32[]{:S(2)}) copy-start(bf16[128,2048]{1,0:T(8,128)(2,1)} %reduce-scatter.2.cloned.1.call-done) | copy-start | bytes 1572868
Sparse Core Ops, SparseCore 0:
  26.7 21.0 all-gather.1
  65.1 31.5 reduce-scatter.1
where the time goes:
time: 313 us; the launch traced here: 312 us
  waiting for transfers between devices  109 us (35%)
  blocking collectives  77.4 us (25%)
  local copies, waits for them, and re-layouts  43.3 us (14%)
  matrix products  33.5 us (11%)
  other arithmetic  26.5 us (8%)
  between operations  14.3 us (5%)
  starting transfers between devices  8.38 us (3%)
    all_to_all x1, blocking collectives, local(): lax.all_to_all(outgoing.reshape(groups, -1, model_width), 'expert', split...  77.4 us
    all_to_all x1, waiting for transfers between devices, local(): lax.all_to_all(produced.reshape(groups, -1, model_width), 'expert', split...  69.9 us
    another operation x3, other arithmetic  18.2 us
    dot_general x1, matrix products, local(): jnp.einsum('sech,ehd->secd', hidden, expert_out[0], preferred_element_typ...  18 us
    ppermute x1, waiting for transfers between devices, passed_along(): return lax.ppermute(block, axis, route)  15.2 us
    gather x1, local copies, waits for them, and re-layouts, local(): picked = returned[jnp.where(active[:, None], slot_index, 0)]  12.6 us
    all_gather x1, waiting for transfers between devices, local(): lax.all_gather(normed, 'expert', axis=0, tiled=True)  12.2 us
    reduce_scatter x1, waiting for transfers between devices, local(): lax.psum_scatter(jnp.dot(attended, out_rows, preferred_element_type=jnp.f...  11.3 us
  transfers between devices with their start and end apart: 4, of which 4 were waited for; matrix products, arithmetic and copies ran while one was open for 9% of the time, Pallas kernels for 0%

commit v1 on v0

v1 whole, which is shorter than its diff:
```python
import jax
import jax.numpy as jnp
from jax import lax
from jax.sharding import PartitionSpec as P

HEAD_SIZE = 128
CAP = 24


EPSILON = 1e-06


def passed_along(block, axis, distance):
    devices = range(lax.axis_size(axis))
    route = [((i - distance) % len(devices), i) for i in devices]
    return lax.ppermute(block, axis, route)


def rms_scale(inputs, gain_row):
    mean_sq = jnp.mean(inputs * inputs, axis=-1, keepdims=True)
    return inputs * lax.rsqrt(mean_sq + EPSILON) * gain_row


def local(
    carried,
    halting,
    section_lap,
    routing,
    attention_gain,
    attention_in,
    attention_out,
    expert_gain,
    router,
    expert_in,
    expert_out,
):
    incoming = passed_along(carried, "section", 1)[0]
    tok_dev = incoming.shape[0]
    model_width = incoming.shape[1]
    groups = lax.axis_size("expert")
    residual = incoming.astype(jnp.float32)
    normed = rms_scale(residual, attention_gain[0]).astype(jnp.bfloat16)
    weights_in = jnp.transpose(attention_in[0], (1, 0, 2))
    head_cols = weights_in.shape[2]
    heads_here = head_cols // HEAD_SIZE
    gathered = lax.all_gather(normed, "expert", axis=0, tiled=True)
    seq_len = gathered.shape[0]
    queries, keys_all, values_all = (
        jnp.dot(gathered, weights_in[part], preferred_element_type=jnp.float32)
        .astype(jnp.bfloat16)
        .reshape(seq_len, heads_here, HEAD_SIZE)
        for part in range(3)
    )
    row_block = min(512, seq_len)

    def attend_block(block_index):
        first_row = block_index * row_block
        query_rows = lax.dynamic_slice_in_dim(queries, first_row, row_block, 0)
        scores = jnp.einsum(
            "qhc,khc->hqk", query_rows, keys_all, preferred_element_type=jnp.float32
        ) * HEAD_SIZE ** (-0.5)
        row_ids = first_row + lax.broadcasted_iota(jnp.int32, (1, row_block, seq_len), 1)
        col_ids = lax.broadcasted_iota(jnp.int32, (1, row_block, seq_len), 2)
        scores = jnp.where(col_ids <= row_ids, scores, -jnp.inf)
        row_max = jnp.max(scores, axis=-1, keepdims=True)
        weights = jnp.exp(scores - row_max)
        weights = (weights / jnp.sum(weights, axis=-1, keepdims=True)).astype(jnp.bfloat16)
        return jnp.einsum(
            "hqk,khc->qhc", weights, values_all, preferred_element_type=jnp.float32
        ).astype(jnp.bfloat16)

    attended = lax.map(attend_block, jnp.arange(seq_len // row_block, dtype=jnp.int32)).reshape(
        seq_len, head_cols
    )
    out_rows = attention_out[0]
    attention_sum = lax.psum_scatter(
        jnp.dot(attended, out_rows, preferred_element_type=jnp.float32).astype(jnp.bfloat16),
        "expert",
        scatter_dimension=0,
        tiled=True,
    ).astype(jnp.float32)
    updated = residual + attention_sum
    expert_input = rms_scale(updated, expert_gain[0]).astype(jnp.bfloat16)
    active = halting[0] >= section_lap[0]
    experts_total = router.shape[2]
    exp_local = expert_in.shape[1]
    routes = jnp.where(active[:, None], routing[0], experts_total).T
    routes_all = lax.all_gather(routes, "expert", axis=0)
    expert_ids = lax.axis_index("expert") * exp_local + jnp.arange(exp_local, dtype=jnp.int32)
    chosen = jnp.any(routes_all[:, :, None, :] == expert_ids[None, None, :, None], axis=1)
    earlier = jnp.triu(jnp.ones((tok_dev, tok_dev), jnp.bfloat16), 1)
    place = jnp.einsum(
        "bet,tu->beu", chosen.astype(jnp.bfloat16), earlier, preferred_element_type=jnp.float32
    ).astype(jnp.int32)
    slots = jnp.where(chosen, place, CAP)[:, :, None, :] == jnp.arange(CAP)[:, None]
    tokens = lax.all_gather(expert_input, "expert", axis=0)
    columns = lax.dynamic_slice_in_dim(router[0].T, expert_ids[0], exp_local, 0)
    gates = jax.nn.sigmoid(
        jnp.einsum("ed,btd->bet", columns, tokens, preferred_element_type=jnp.float32)
    )
    packed = jnp.einsum(
        "bect,btd->ebcd", slots.astype(jnp.bfloat16), tokens, preferred_element_type=jnp.bfloat16
    ).reshape(exp_local, groups * CAP, model_width)
    hidden = jax.nn.relu(
        jnp.einsum("ecd,edh->ech", packed, expert_in[0], preferred_element_type=jnp.float32)
    ).astype(jnp.bfloat16)
    produced = jnp.einsum(
        "ech,ehd->ecd", hidden, expert_out[0], preferred_element_type=jnp.float32
    ).astype(jnp.bfloat16)
    produced = produced.reshape(exp_local, groups, CAP, model_width)
    weight = jnp.where(slots, gates[:, :, None, :], 0.0)
    coarse = lax.reduce_precision(weight, 8, 7)
    fine = (weight - coarse).astype(jnp.bfloat16)
    partial = sum(
        jnp.einsum("bect,ebcd->btd", part, produced, preferred_element_type=jnp.float32)
        for part in (coarse.astype(jnp.bfloat16), fine)
    )
    expert_sum = lax.psum_scatter(
        partial.astype(jnp.bfloat16).reshape(-1, model_width),
        "expert",
        scatter_dimension=0,
        tiled=True,
    ).astype(jnp.float32)
    stepped = jnp.where(active[:, None], updated + expert_sum, residual).astype(jnp.bfloat16)
    return stepped[None]


def solution(mesh):
    in_specs = (
        P("section", "expert", None),
        P("section", "expert"),
        P("section"),
        P("section", "expert", None),
        P("section", None),
        P("section", None, None, "expert"),
        P("section", "expert", None),
        P("section", None),
        P("section", None, None),
        P("section", "expert", None, None),
        P("section", "expert", None, None),
    )
    out_specs = P("section", "expert", None)
    return jax.shard_map(local, mesh=mesh, in_specs=in_specs, out_specs=out_specs, check_vma=False)
```

time: 313 us -> 200 us (0.64)
  blocking collectives: 77.4 us -> 5.37 us
  local copies, waits for them, and re-layouts: 43.3 us -> 3.62 us
  other arithmetic: 26.5 us -> 7.57 us
  matrix products: 33.5 us -> 50.6 us
  waiting for transfers between devices: 109 us -> 116 us
  starting transfers between devices: 8.38 us -> 3.09 us
    all_to_all x1 -> x0, blocking collectives: 77.4 us -> none  [local(): lax.all_to_all(outgoing.reshape(groups, -1, model_width), 'expert', split...]
    all_to_all x1 -> x0, waiting for transfers between devices: 69.9 us -> none  [local(): lax.all_to_all(produced.reshape(groups, -1, model_width), 'expert', split...]
    reduce_scatter x0 -> x1, waiting for transfers between devices: none -> 31.5 us  [local(): lax.psum_scatter(partial.astype(jnp.bfloat16).reshape(-1, model_width), '...]
    all_gather x1 -> x2, waiting for transfers between devices: 12.2 us -> 37.4 us  [the longest x1 21 us: local(): gathered = lax.all_gather(normed, 'expert', axis=0, tiled=True)]
    reduce_scatter x1, waiting for transfers between devices: 11.3 us -> 31.5 us  [local(): lax.psum_scatter(jnp.dot(attended, out_rows, preferred_element_type=jnp.f...]
    another operation x3 -> x0, other arithmetic: 18.2 us -> none
    gather x1 -> x0, local copies, waits for them, and re-layouts: 12.6 us -> none  [local(): picked = returned[jnp.where(active[:, None], slot_index, 0)]]
    dot_general x5 -> x9, matrix products: 30.4 us -> 42.9 us  [the longest x1 19.9 us: local(): jnp.einsum('ech,ehd->ecd', hidden, expert_out[0], preferred_element_type=...]
  transfers between devices with their start and end apart: 4 -> 5, of which waited for: 4 -> 5; matrix products, arithmetic and copies ran while one was open for 9% -> 0% of each run, Pallas kernels for 0% -> 0%
where the time goes in v1:
time: 200 us
  waiting for transfers between devices  116 us (58%)
  matrix products  50.6 us (25%)
  between operations  14.1 us (7%)
  other arithmetic  7.57 us (4%)
  blocking collectives  5.37 us (3%)
  local copies, waits for them, and re-layouts  3.62 us (2%)
  starting transfers between devices  3.09 us (2%)
    reduce_scatter x1, waiting for transfers between devices, local(): lax.psum_scatter(jnp.dot(attended, out_rows, preferred_element_type=jnp.f...  31.5 us
    reduce_scatter x1, waiting for transfers between devices, local(): lax.psum_scatter(partial.astype(jnp.bfloat16).reshape(-1, model_width), '...  31.5 us
    all_gather x1, waiting for transfers between devices, local(): gathered = lax.all_gather(normed, 'expert', axis=0, tiled=True)  21 us
    dot_general x1, matrix products, local(): jnp.einsum('ech,ehd->ecd', hidden, expert_out[0], preferred_element_type=...  19.9 us
    all_gather x1, waiting for transfers between devices, local(): tokens = lax.all_gather(expert_input, 'expert', axis=0)  16.4 us
    ppermute x1, waiting for transfers between devices, passed_along(): return lax.ppermute(block, axis, route)  15.2 us
    dot_general x3, matrix products, local(): jnp.dot(gathered, weights_in[part], preferred_element_type=jnp.float32)  11 us
    dot_general x2, matrix products, local(): jnp.einsum('bect,ebcd->btd', part, produced, preferred_element_type=jnp.f...  6.92 us
  transfers between devices with their start and end apart: 5, of which 5 were waited for; matrix products, arithmetic and copies ran while one was open for 0% of the time, Pallas kernels for 0%

profile of v1, /device:TPU:0, one launch (start us, length us, event | category | flops | bytes accessed | tf_op | source)
XLA Modules:
  0.0 199.9 jit_solution(12927566563689948095)
XLA Ops:
  6.5 0.0 copy-start
  6.5 0.0 all-gather.5.cloned.1.call-start
  6.5 3.0 %collective-permute-start = (bf16[1,128,2048]{2,1,0:T(8,128)(2,1)}, bf16[1,128,2048]{2,1,0:T(8,128)(2,1)S(1)}, u32[]{:S(2)}, u32[]{:S(2)}) collective-permute-start(bf16[1,128,2048]{2,1,0:T(8,128)(2,1)} %param.11), channel_id=1, source_target_pairs={{28,0},{0,4},{4,8},{8,12},{12,16},{16,20},{20,24},{24,28},{29,1},{... | collective-permute-start | bytes 1572872 | tf_op jit(solution)/shard_map/ppermute | solution.py:16
  9.5 15.2 %collective-permute-done = bf16[1,128,2048]{2,1,0:T(8,128)(2,1)S(1)} collective-permute-done((bf16[1,128,2048]{2,1,0:T(8,128)(2,1)}, bf16[1,128,2048]{2,1,0:T(8,128)(2,1)S(1)}, u32[]{:S(2)}, u32[]{:S(2)}) %collective-permute-start) | collective-permute-done | bytes 524320 | tf_op jit(solution)/shard_map/ppermute | solution.py:16
  24.7 0.2 fusion.37
  24.9 1.7 fusion.39
  26.6 0.0 all-gather.5.cloned.1.call-update
  26.6 0.0 reduce-scatter.3.cloned.1.call-start
  26.6 0.1 iota_compare_fusion
  26.7 21.0 %all-gather.5.cloned.1.call-done = bf16[512,2048]{1,0:T(8,128)(2,1)} async-done(((bf16[128,2048]{1,0:T(8,128)(2,1)}), bf16[512,2048]{1,0:T(8,128)(2,1)}) %all-gather.5.cloned.1.call-update) | async-done | bytes 2097168 | tf_op jit(solution)/shard_map/all_gather | solution.py:46
  47.8 3.7 %fusion.26 = bf16[512,512]{0,1:T(8,128)(2,1)S(1)} fusion(bf16[512,2048]{1,0:T(8,128)(2,1)} %all-gather.5.cloned.1.call-done, bf16[3,2048,512]{2,1,0:T(8,128)(2,1)} %bitcast.115), kind=kOutput, calls=%fused_computation.36 | convolution fusion | flops 1074003968 | bytes 4718592 | tf_op jit(solution)/shard_map/dot_general | solution.py:49
  51.4 0.0 copy-done.7
  51.4 3.7 %fusion.25 = bf16[512,512]{0,1:T(8,128)(2,1)} fusion(bf16[512,2048]{1,0:T(8,128)(2,1)S(1)} %copy-done.7, bf16[3,2048,512]{2,1,0:T(8,128)(2,1)} %bitcast.116), kind=kOutput, calls=%fused_computation.35 | convolution fusion | flops 1074003968 | bytes 4718592 | tf_op jit(solution)/shard_map/dot_general | solution.py:49
  55.1 4.6 %fusion.70 = (f32[4,512]{1,0:T(4,128)S(1)}, f32[4,512,512]{1,2,0:T(8,128)}) fusion(pred[512,512]{0,1:T(8,128)(4,1)S(1)} %iota_compare_fusion, bf16[512,4,128]{0,2,1:T(8,128)(2,1)} %bitcast.119, bf16[512,4,128]{0,2,1:T(8,128)(2,1)S(1)} %bitcast.118), kind=kOutput, calls=%fused_computation.88 | convolution fusion | flops 272630272 | bytes 5513216 | tf_op jit(solution)/shard_map/while/body/eval_jaxpr/sub | solution.py:66
  59.8 3.7 %fusion.24 = bf16[512,512]{0,1:T(8,128)(2,1)S(1)} fusion(bf16[512,2048]{1,0:T(8,128)(2,1)} %all-gather.5.cloned.1.call-done, bf16[3,2048,512]{2,1,0:T(8,128)(2,1)} %bitcast.117), kind=kOutput, calls=%fused_computation.34 | convolution fusion | flops 1074003968 | bytes 4718592 | tf_op jit(solution)/shard_map/dot_general | solution.py:49
  63.5 0.0 copy-done.9
  63.5 0.5 fusion.27
  63.9 0.0 copy-done
  63.9 0.0 copy-start.5
  64.0 0.0 copy-start.8
  64.0 0.0 copy-start.6
  64.0 2.6 %convolution_convert_fusion = bf16[512,2048]{1,0:T(8,128)(2,1)} fusion(bf16[512,512]{0,1:T(8,128)(2,1)S(1)} %bitcast.121, bf16[1,512,2048]{2,1,0:T(8,128)(2,1)S(1)} %copy-done), kind=kOutput, calls=%fused_computation.17 | convolution fusion | flops 1074790400 | bytes 4718592 | tf_op jit(solution)/shard_map/dot_general | solution.py:77
  66.6 0.0 reduce-scatter.3.cloned.1.call-update
  66.6 0.0 all-gather.7.cloned.1.call-start
  66.7 31.5 %reduce-scatter.3.cloned.1.call-done = bf16[128,2048]{1,0:T(8,128)(2,1)} async-done(((bf16[512,2048]{1,0:T(8,128)(2,1)}), bf16[128,2048]{1,0:T(8,128)(2,1)}) %reduce-scatter.3.cloned.1.call-update) | async-done | bytes 524304 | tf_op jit(solution)/shard_map/reduce_scatter | solution.py:76
  98.2 1.3 multiply_reduce_fusion
  99.5 0.0 copy-done.5
  99.5 2.0 %multiply_convert_fusion = bf16[128,2048]{1,0:T(8,128)(2,1)} fusion(bf16[128,2048]{1,0:T(8,128)(2,1)} %reduce-scatter.3.cloned.1.call-done, bf16[1,128,2048]{2,1,0:T(8,128)(2,1)S(1)} %collective-permute-done, f32[2048]{0:T(1024)S(1)} %bitcast.111, f32[128]{0:T(128)S(1)} %add_rsqrt_fusion), kind=kLoop, calls=%fused_computation.51 | loop fusion | flops 1572864 | bytes 1581568 | tf_op jit(solution)/shard_map/convert_element_type | solution.py:83
  101.5 0.0 all-gather.7.cloned.1.call-update
  101.6 0.0 reduce-scatter.5.cloned.1.call-start
  102.4 0.0 copy-done.8
  102.4 0.0 copy-done.6
  102.4 5.4 %all-gather = s32[32,128]{1,0:T(8,128)S(1)} all-gather(s32[8,128]{1,0:T(8,128)S(1)} %fusion.61), channel_id=2, replica_groups=mesh['section'=8,'expert'=4] {'expert'}, dimensions={0}, use_global_device_ids=true | all-gather | bytes 20480 | tf_op jit(solution)/shard_map/all_gather | solution.py:88
  107.8 0.1 compare_reduce_fusion
  107.9 0.1 fusion.36
  108.0 16.4 %all-gather.7.cloned.1.call-done = bf16[512,2048]{1,0:T(8,128)(2,1)} async-done(((bf16[128,2048]{1,0:T(8,128)(2,1)}), bf16[512,2048]{1,0:T(8,128)(2,1)}) %all-gather.7.cloned.1.call-update) | async-done | bytes 2097168 | tf_op jit(solution)/shard_map/all_gather | solution.py:96
  124.4 3.4 %convolution_bitcast_fusion = bf16[16,4,24,2048]{3,2,0,1:T(8,128)(2,1)S(1)} fusion(bf16[4,128,2048,1]{2,1,3,0:T(8,128)(2,1)} %bitcast.107, s32[4,16,128]{2,1,0:T(8,128)S(1)} %fusion.36), kind=kOutput, calls=%fused_computation.15 | convolution fusion | flops 805502976 | bytes 8421376 | tf_op jit(solution)/shard_map/bect,btd->ebcd/dot_general | solution.py:101
  127.8 0.0 copy-start.4
  127.8 3.2 %copy.26 = bf16[16,4,24,2048]{3,2,1,0:T(8,128)(2,1)} copy(bf16[16,4,24,2048]{3,2,0,1:T(8,128)(2,1)S(1)} %convolution_bitcast_fusion) | data formatting | bytes 12582912 | tf_op jit(solution)/shard_map/bect,btd->ebcd/transpose | solution.py:101
  131.0 0.0 copy-done.4
  131.0 1.6 fusion.35
  132.6 19.9 %fusion.9 = bf16[16,96,2048]{2,1,0:T(8,128)(2,1)} fusion(bf16[1,16,256,2048]{3,2,1,0:T(8,128)(2,1)} %param.21, bf16[16,96,2048]{2,1,0:T(8,128)(2,1)} %bitcast.105, bf16[1,16,2048,256]{3,2,1,0:T(8,128)(2,1)} %param.20), kind=kOutput, calls=%fused_computation.9 | convolution fusion | flops 3225157632 | bytes 46137344 | tf_op jit(solution)/shard_map/ech,ehd->ecd/dot_general | solution.py:107
  152.5 4.2 %fusion.5 = f32[4,128,2048,1]{2,1,3,0:T(8,128)S(1)} fusion(bf16[16,4,24,2048]{3,2,1,0:T(8,128)(2,1)} %bitcast.103, f32[4,16,128]{2,1,0:T(8,128)S(1)} %fusion.35, s32[4,16,128]{2,1,0:T(8,128)S(1)} %fusion.36), kind=kOutput, calls=%fused_computation.5 | convolution fusion | flops 806289408 | bytes 10551296 | tf_op jit(solution)/shard_map/bect,ebcd->btd/dot_general | solution.py:115
  156.7 0.3 copy-done.2
  157.1 2.7 %fusion.12 = bf16[4,128,2048]{2,1,0:T(8,128)(2,1)} fusion(f32[4,128,2048,1]{2,1,3,0:T(8,128)S(1)} %fusion.5, bf16[16,4,24,2048]{3,2,1,0:T(8,128)(2,1)S(1)} %bitcast.104, f32[4,16,128]{2,1,0:T(8,128)S(1)} %fusion.35, s32[4,16,128]{2,1,0:T(8,128)S(1)} %fusion.36), kind=kOutput, calls=%fused_computation.11 | convolution fusion | flops 808189952 | bytes 12648448 | tf_op jit(solution)/shard_map/bect,ebcd->btd/dot_general | solution.py:115
  159.8 0.0 reduce-scatter.5.cloned.1.call-update
  159.8 31.5 %reduce-scatter.5.cloned.1.call-done = bf16[128,2048]{1,0:T(8,128)(2,1)} async-done(((bf16[512,2048]{1,0:T(8,128)(2,1)}), bf16[128,2048]{1,0:T(8,128)(2,1)}) %reduce-scatter.5.cloned.1.call-update) | async-done | bytes 524304 | tf_op jit(solution)/shard_map/reduce_scatter | solution.py:118
  191.2 2.2 %fusion.43 = bf16[1,128,2048]{2,1,0:T(8,128)(2,1)} fusion(bf16[128,2048]{1,0:T(8,128)(2,1)} %reduce-scatter.5.cloned.1.call-done, bf16[128,2048]{1,0:T(8,128)(2,1)S(1)} %copy-done.3, bf16[1,128,2048]{2,1,0:T(8,128)(2,1)S(1)} %collective-permute-done, pred[128]{0:T(512)(128)(4,1)S(1)} %compare_bitcast_fusion), kind=kLoop, calls=%fused_computation.57 | loop fusion | flops 1835008 | bytes 2097280 | tf_op jit(solution)/shard_map/broadcast_in_dim | solution.py:125
  (12 shorter events, 0.0 us)
Async XLA Ops:
  6.5 57.4 %copy-start = (bf16[1,512,2048]{2,1,0:T(8,128)(2,1)S(1)}, bf16[1,512,2048]{2,1,0:T(8,128)(2,1)}, u32[]{:S(2)}) copy-start(bf16[1,512,2048]{2,1,0:T(8,128)(2,1)} %param.17) | copy-start | bytes 6291460
  6.5 41.2 %all-gather.5.cloned.1.call-start = ((), (), s32[]{:S(2)}) async-start(), calls=%async_computation.2 | async-start | bytes 2621440 | tf_op jit(solution)/shard_map/all_gather | solution.py:46
  6.5 18.1 %collective-permute-start = (bf16[1,128,2048]{2,1,0:T(8,128)(2,1)}, bf16[1,128,2048]{2,1,0:T(8,128)(2,1)S(1)}, u32[]{:S(2)}, u32[]{:S(2)}) collective-permute-start(bf16[1,128,2048]{2,1,0:T(8,128)(2,1)} %param.11), channel_id=1, source_target_pairs={{28,0},{0,4},{4,8},{8,12},{12,16},{16,20},{20,24},{24,28},{29,1},{... | collective-permute-start | bytes 1572872 | tf_op jit(solution)/shard_map/ppermute | solution.py:16
  26.6 71.6 %reduce-scatter.3.cloned.1.call-start = ((), (), s32[]{:S(2)}) async-start(), calls=%async_computation.3 | async-start | bytes 2621440 | tf_op jit(solution)/shard_map/reduce_scatter | solution.py:76
  47.8 3.7 %copy-start.7 = (bf16[512,2048]{1,0:T(8,128)(2,1)S(1)}, bf16[512,2048]{1,0:T(8,128)(2,1)}, u32[]{:S(2)}) copy-start(bf16[512,2048]{1,0:T(8,128)(2,1)} %all-gather.5.cloned.1.call-done) | copy-start | bytes 6291460
  59.8 3.7 %copy-start.9 = (f32[4,512,512]{1,2,0:T(8,128)S(1)}, f32[4,512,512]{1,2,0:T(8,128)}, u32[]{:S(2)}) copy-start(f32[4,512,512]{1,2,0:T(8,128)} %get-tuple-element.14) | copy-start | bytes 12582916
  63.9 35.6 %copy-start.5 = (f32[1,2048]{1,0:T(1,128)S(1)}, f32[1,2048]{1,0:T(1,128)}, u32[]{:S(2)}) copy-start(f32[1,2048]{1,0:T(1,128)} %param.18) | copy-start | bytes 24580
  64.0 38.4 %copy-start.8 = (s32[1,128]{1,0:T(1,128)S(1)}, s32[1,128]{1,0:T(1,128)}, u32[]{:S(2)}) copy-start(s32[1,128]{1,0:T(1,128)} %param.12) | copy-start | bytes 1540
  64.0 38.4 %copy-start.6 = (s32[1,128,8]{1,2,0:T(8,128)S(1)}, s32[1,128,8]{1,2,0:T(8,128)}, u32[]{:S(2)}) copy-start(s32[1,128,8]{1,2,0:T(8,128)} %param.14) | copy-start | bytes 12292
  66.6 57.8 %all-gather.7.cloned.1.call-start = ((), (), s32[]{:S(2)}) async-start(), calls=%async_computation.5 | async-start | bytes 2621440 | tf_op jit(solution)/shard_map/all_gather | solution.py:96
  101.6 89.7 %reduce-scatter.5.cloned.1.call-start = ((), (), s32[]{:S(2)}) async-start(), calls=%async_computation.4 | async-start | bytes 2621440 | tf_op jit(solution)/shard_map/reduce_scatter | solution.py:118
  127.8 3.2 %copy-start.4 = (bf16[512,2048]{1,0:T(8,128)(2,1)S(1)}, bf16[512,2048]{1,0:T(8,128)(2,1)}, u32[]{:S(2)}) copy-start(bf16[512,2048]{1,0:T(8,128)(2,1)} %all-gather.7.cloned.1.call-done) | copy-start | bytes 6291460
  152.5 4.6 %copy-start.2 = (bf16[16,96,2048]{2,1,0:T(8,128)(2,1)S(1)}, bf16[16,96,2048]{2,1,0:T(8,128)(2,1)}, u32[]{:S(2)}) copy-start(bf16[16,96,2048]{2,1,0:T(8,128)(2,1)} %fusion.9) | copy-start | bytes 18874372
  157.1 34.2 %copy-start.3 = (bf16[128,2048]{1,0:T(8,128)(2,1)S(1)}, bf16[128,2048]{1,0:T(8,128)(2,1)}, u32[]{:S(2)}) copy-start(bf16[128,2048]{1,0:T(8,128)(2,1)} %reduce-scatter.3.cloned.1.call-done) | copy-start | bytes 1572868
  157.1 36.3 %copy-start.1 = (bf16[1,512,2048]{2,1,0:T(8,128)(2,1)S(1)}, bf16[1,512,2048]{2,1,0:T(8,128)(2,1)}, u32[]{:S(2)}) copy-start(bf16[1,512,2048]{2,1,0:T(8,128)(2,1)} %param.17) | copy-start | bytes 6291460
Sparse Core Ops, SparseCore 0:
  26.7 21.0 all-gather.4
  66.7 31.4 reduce-scatter.2
  101.7 22.7 all-gather.6
  159.9 31.2 reduce-scatter.4

commit v2 on v1

--- a/solution.py
+++ b/solution.py
@@ -1,6 +1,8 @@
 import jax
 import jax.numpy as jnp
 from jax import lax
+from jax.experimental import pallas as pl
+from jax.experimental.pallas import tpu as pltpu
 from jax.sharding import PartitionSpec as P
 
 HEAD_SIZE = 128
@@ -21,7 +23,7 @@
     return inputs * lax.rsqrt(mean_sq + EPSILON) * gain_row
 
 
-def local(
+def local_general(
     carried,
     halting,
     section_lap,
@@ -125,6 +127,345 @@
     return stepped[None]
 
 
+CHUNKS = 4
+SLOT = 32
+F32 = jnp.float32
+BF16 = jnp.bfloat16
+
+
+def tick_kernel(
+    carried, choice, active, gain_a, gain_e, columns, w_in, w_out, e_in, e_out, out,
+    vw_in, vw_out, ve_in, ve_out, packed, incoming, tokens, updated, qkv, heads,
+    stage, from_sib, from_cnt, weight, choices,
+    load_sem, hop_s, hop_r, gather_s, gather_r, sum_s, sum_r, choice_s, choice_r,
+):
+    me = lax.axis_index("expert")
+    section, sections = lax.axis_index("section"), lax.axis_size("section")
+    sib = me + 1 - 2 * lax.rem(me, 2)
+    cnt = me + 2 - 4 * (me // 2)
+    dia = sib + 2 - 4 * (sib // 2)
+    after, ahead = lax.rem(section + 1, sections), lax.rem(section + sections - 1, sections)
+    exp_local, width = e_in.shape[0], e_in.shape[1]
+    rows = tokens.shape[2]
+    block = CHUNKS * rows
+
+    loads = [
+        pltpu.make_async_copy(w_in, vw_in, load_sem.at[0]),
+        pltpu.make_async_copy(w_out, vw_out, load_sem.at[1]),
+        pltpu.make_async_copy(e_in, ve_in, load_sem.at[2]),
+        pltpu.make_async_copy(e_out, ve_out, load_sem.at[3]),
+    ]
+    loads[0].start()
+    loads[1].start()
+
+    barrier = pltpu.get_barrier_semaphore()
+    for peer in (sib, cnt, dia):
+        pl.semaphore_signal(barrier, inc=1, device_id={"expert": peer})
+    for peer in (after, ahead):
+        pl.semaphore_signal(barrier, inc=1, device_id={"section": peer})
+    pl.semaphore_wait(barrier, 5)
+
+    hops = [
+        pltpu.make_async_remote_copy(
+            src_ref=carried.at[c], dst_ref=incoming.at[c], send_sem=hop_s.at[c],
+            recv_sem=hop_r.at[c], device_id={"section": after},
+        )
+        for c in range(CHUNKS)
+    ]
+    for hop in hops:
+        hop.start()
+    shared = []
+    for i, peer in enumerate((sib, cnt, dia)):
+        shared.append(
+            pltpu.make_async_remote_copy(
+                src_ref=choice, dst_ref=choices.at[me], send_sem=choice_s.at[i],
+                recv_sem=choice_r.at[i], device_id={"expert": peer},
+            )
+        )
+        shared[-1].start()
+    choices[me] = choice[...]
+    loads[2].start()
+    loads[3].start()
+
+    def spread(phase, c, kind):
+        source, peer = ((me, sib), (me, cnt), (cnt, sib))[kind]
+        return pltpu.make_async_remote_copy(
+            src_ref=tokens.at[source, c], dst_ref=tokens.at[source, c],
+            send_sem=gather_s.at[phase, kind, c], recv_sem=gather_r.at[phase, kind, c],
+            device_id={"expert": peer},
+        )
+
+    def normed(values, gain):
+        mean_sq = jnp.mean(values * values, axis=-1, keepdims=True)
+        return (values * lax.rsqrt(mean_sq + EPSILON) * gain[...]).astype(BF16)
+
+    def pass_on(phase):
+        for c in range(CHUNKS):
+            spread(phase, c, 1).wait_recv()
+            spread(phase, c, 2).start()
+
+    def sent(phase):
+        for c in range(CHUNKS):
+            for kind in range(3):
+                spread(phase, c, kind).wait_send()
+
+    for c in range(CHUNKS):
+        hops[c].wait_recv()
+        tokens[me, c] = normed(incoming[c].astype(F32), gain_a)
+        spread(0, c, 0).start()
+        spread(0, c, 1).start()
+    pass_on(0)
+    for kind in (0, 2):
+        for c in range(CHUNKS):
+            spread(0, c, kind).wait_recv()
+    loads[0].wait()
+    n = tokens.shape[0]
+    seq = n * block
+
+    @pl.loop(0, qkv.shape[0])
+    def _(tile):
+        cols = pl.ds(pl.multiple_of(lax.rem(tile, 2) * 256, 256), 256)
+        qkv[tile] = jnp.dot(
+            tokens[...].reshape(seq, width), vw_in[tile // 2, :, cols],
+            preferred_element_type=F32,
+        ).astype(BF16)
+
+    span = 256
+
+    @pl.loop(0, heads.shape[1] // HEAD_SIZE)
+    def _(head):
+        cols = pl.ds(pl.multiple_of(lax.rem(head, 2) * HEAD_SIZE, HEAD_SIZE), HEAD_SIZE)
+        place = pl.ds(pl.multiple_of(head * HEAD_SIZE, HEAD_SIZE), HEAD_SIZE)
+        for first in range(0, seq, span):
+            upto = first + span
+            query = qkv[head // 2, first:upto, cols]
+            key = qkv[2 + head // 2, :upto, cols]
+            value = qkv[4 + head // 2, :upto, cols]
+            scores = lax.dot_general(
+                query, key, (((1,), (1,)), ((), ())), preferred_element_type=F32
+            ) * HEAD_SIZE ** (-0.5)
+            row_ids = first + lax.broadcasted_iota(jnp.int32, scores.shape, 0)
+            col_ids = lax.broadcasted_iota(jnp.int32, scores.shape, 1)
+            scores = jnp.where(col_ids <= row_ids, scores, -jnp.inf)
+            powers = jnp.exp(scores - jnp.max(scores, axis=-1, keepdims=True))
+            shares = (powers / jnp.sum(powers, axis=-1, keepdims=True)).astype(BF16)
+            heads[first:upto, place] = jnp.dot(
+                shares, value, preferred_element_type=F32
+            ).astype(BF16)
+
+    sent(0)
+    loads[1].wait()
+    wide = 512
+
+    def reduce_blocks(phase, term, box, buffers):
+        to_sib, to_cnt, to_sib_own = buffers
+        box_dia, box_sib, box_cnt = box
+        moves = []
+
+        def move(kind, c, source, target, peer):
+            copy = pltpu.make_async_remote_copy(
+                src_ref=source, dst_ref=target, send_sem=sum_s.at[phase, kind, c],
+                recv_sem=sum_r.at[phase, kind, c], device_id={"expert": peer},
+            )
+            copy.start()
+            moves.append(copy)
+            return copy
+
+        def fill(target, number):
+            @pl.loop(0, width // wide)
+            def _(j):
+                cols = pl.ds(pl.multiple_of(j * wide, wide), wide)
+                target[:, :, cols] = term(number, cols).astype(BF16).reshape(CHUNKS, rows, wide)
+
+        fill(to_sib, dia)
+        first = move(0, 0, to_sib, box_dia, sib)
+        fill(to_cnt, cnt)
+        first.wait_recv()
+        across = []
+        for c in range(CHUNKS):
+            to_cnt[c] = (to_cnt[c].astype(F32) + box_dia[c].astype(F32)).astype(BF16)
+            across.append(move(1, c, to_cnt.at[c], box_cnt.at[c], cnt))
+        fill(to_sib_own, sib)
+        beside = move(2, 0, to_sib_own, box_sib, sib)
+        return moves, across, beside
+
+    def out_term(number, cols):
+        mine = heads[pl.ds(pl.multiple_of(number * block, block), block), :]
+        return jnp.dot(mine, vw_out[:, cols], preferred_element_type=F32)
+
+    moves, across, beside = reduce_blocks(
+        0, out_term, (stage.at[0], from_sib.at[0], from_cnt.at[0]),
+        (packed.at[0], packed.at[1], packed.at[2]),
+    )
+
+    @pl.loop(0, width // wide)
+    def _(j):
+        cols = pl.ds(pl.multiple_of(j * wide, wide), wide)
+        own = out_term(me, cols).astype(BF16).astype(F32)
+        updated[:, :, cols] = incoming[:, :, cols].astype(F32) + own.reshape(CHUNKS, rows, wide)
+
+    beside.wait_recv()
+    for c in range(CHUNKS):
+        across[c].wait_recv()
+        total = updated[c] + (from_sib[0, c].astype(F32) + from_cnt[0, c].astype(F32))
+        updated[c] = total
+        tokens[me, c] = normed(total, gain_e)
+        spread(1, c, 0).start()
+        spread(1, c, 1).start()
+    for copy in moves:
+        copy.wait_send()
+    for copy in shared:
+        copy.wait()
+    for hop in hops:
+        hop.wait_send()
+
+    def dispatch(b):
+        names = choices[b]
+        own = tokens[b].reshape(block, width)
+        gates = jax.nn.sigmoid(
+            lax.dot_general(
+                columns[...], own, (((1,), (1,)), ((), ())), preferred_element_type=F32
+            )
+        )
+        ids = me * exp_local + lax.broadcasted_iota(jnp.int32, (exp_local, block), 0)
+        hit = jnp.zeros((exp_local, block), F32)
+        for k in range(names.shape[0]):
+            hit = hit + jnp.where(names[k : k + 1, :] == ids, 1.0, 0.0)
+        earlier = jnp.where(
+            lax.broadcasted_iota(jnp.int32, (block, block), 0)
+            < lax.broadcasted_iota(jnp.int32, (block, block), 1), 1.0, 0.0,
+        ).astype(BF16)
+        place = jnp.dot(hit.astype(BF16), earlier, preferred_element_type=F32)
+        place = jnp.where(hit > 0.5, place, -1.0)
+        slot = lax.broadcasted_iota(jnp.int32, (exp_local, SLOT, block), 1).astype(F32)
+        match = place[:, None, :] == slot
+        chosen = jnp.where(match, 1.0, 0.0).reshape(exp_local * SLOT, block).astype(BF16)
+        scale = jnp.where(match, gates[:, None, :], 0.0).reshape(exp_local * SLOT, block)
+        coarse = scale.astype(BF16)
+        weight[b, 0] = coarse
+        weight[b, 1] = (scale - coarse.astype(F32)).astype(BF16)
+
+        @pl.loop(0, width // wide)
+        def _(j):
+            cols = pl.ds(pl.multiple_of(j * wide, wide), wide)
+            picked = jnp.dot(
+                chosen, tokens[b, :, :, cols].reshape(block, wide), preferred_element_type=F32
+            )
+            packed[:, b, :, cols] = picked.astype(BF16).reshape(exp_local, SLOT, wide)
+
+    dispatch(me)
+    pass_on(1)
+    for c in range(CHUNKS):
+        spread(1, c, 0).wait_recv()
+    dispatch(sib)
+    dispatch(cnt)
+    for c in range(CHUNKS):
+        spread(1, c, 2).wait_recv()
+    dispatch(dia)
+    loads[2].wait()
+    loads[3].wait()
+
+    @pl.loop(0, exp_local)
+    def _(e):
+        arrived = packed[e].reshape(n * SLOT, width)
+        hidden = jnp.maximum(jnp.dot(arrived, ve_in[e], preferred_element_type=F32), 0.0)
+        made = jnp.dot(hidden.astype(BF16), ve_out[e], preferred_element_type=F32)
+        packed[e] = made.astype(BF16).reshape(n, SLOT, width)
+
+    sent(1)
+
+    def expert_term(number, cols):
+        made = packed[:, number, :, cols].reshape(exp_local * SLOT, wide)
+        contract = (((0,), (0,)), ((), ()))
+        return lax.dot_general(
+            weight[number, 0], made, contract, preferred_element_type=F32
+        ) + lax.dot_general(weight[number, 1], made, contract, preferred_element_type=F32)
+
+    moves, across, beside = reduce_blocks(
+        1, expert_term, (stage.at[1], from_sib.at[1], from_cnt.at[1]),
+        (stage.at[0], from_cnt.at[0], from_sib.at[0]),
+    )
+
+    @pl.loop(0, width // wide)
+    def _(j):
+        cols = pl.ds(pl.multiple_of(j * wide, wide), wide)
+        updated[:, :, cols] += expert_term(me, cols).reshape(CHUNKS, rows, wide)
+
+    beside.wait_recv()
+    for c in range(CHUNKS):
+        across[c].wait_recv()
+        total = updated[c] + (from_sib[1, c].astype(F32) + from_cnt[1, c].astype(F32))
+        out[c] = jnp.where(active[c] > 0, total, incoming[c].astype(F32)).astype(BF16)
+    for copy in moves:
+        copy.wait_send()
+
+
+def local_fused(
+    carried, halting, section_lap, routing, attention_gain, attention_in, attention_out,
+    expert_gain, router, expert_in, expert_out,
+):
+    tok_dev, width = carried.shape[1:]
+    rows = tok_dev // CHUNKS
+    n = lax.axis_size("expert")
+    exp_local, _, hid = expert_in.shape[1:]
+    active = halting[0] >= section_lap[0]
+    choice = jnp.where(active[None, :], routing[0].T, -1)
+    columns = lax.dynamic_slice_in_dim(
+        router[0].T, lax.axis_index("expert") * exp_local, exp_local, 0
+    )
+    weights_in = jnp.transpose(attention_in[0], (1, 0, 2))
+    cols = weights_in.shape[2]
+    seq = n * tok_dev
+    vmem, far = pl.BlockSpec(memory_space=pltpu.VMEM), pl.BlockSpec(memory_space=pl.ANY)
+    tile = (CHUNKS, rows, width)
+    dma = pltpu.SemaphoreType.DMA
+    result = pl.pallas_call(
+        tick_kernel,
+        out_shape=jax.ShapeDtypeStruct(tile, BF16),
+        in_specs=[far] + [vmem] * 5 + [far] * 4,
+        out_specs=vmem,
+        scratch_shapes=[
+            pltpu.VMEM(weights_in.shape, BF16),
+            pltpu.VMEM((cols, width), BF16),
+            pltpu.VMEM((exp_local, width, hid), BF16),
+            pltpu.VMEM((exp_local, hid, width), BF16),
+            pltpu.VMEM((exp_local, n, SLOT, width), BF16),
+            pltpu.VMEM(tile, BF16),
+            pltpu.VMEM((n,) + tile, BF16),
+            pltpu.VMEM(tile, F32),
+            pltpu.VMEM((3 * cols // 256, seq, 256), BF16),
+            pltpu.VMEM((seq, cols), BF16),
+            pltpu.VMEM((2,) + tile, BF16),
+            pltpu.VMEM((2,) + tile, BF16),
+            pltpu.VMEM((2,) + tile, BF16),
+            pltpu.VMEM((n, 2, exp_local * SLOT, tok_dev), BF16),
+            pltpu.VMEM((n,) + choice.shape, jnp.int32),
+            dma((4,)), dma((CHUNKS,)), dma((CHUNKS,)),
+            dma((2, 3, CHUNKS)), dma((2, 3, CHUNKS)),
+            dma((2, 3, CHUNKS)), dma((2, 3, CHUNKS)),
+            dma((3,)), dma((3,)),
+        ],
+        compiler_params=pltpu.CompilerParams(
+            collective_id=0, has_side_effects=True, vmem_limit_bytes=62 * 1024 * 1024
+        ),
+        cost_estimate=pl.CostEstimate(
+            flops=10 * 10**9, bytes_accessed=45 * 10**6, transcendentals=10**6
+        ),
+    )(
+        carried[0].reshape(tile),
+        choice,
+        active.astype(jnp.int32).reshape(CHUNKS, rows, 1),
+        attention_gain,
+        expert_gain,
+        columns,
+        weights_in,
+        attention_out[0],
+        expert_in[0],
+        expert_out[0],
+    )
+    return result.reshape(1, tok_dev, width)
+
+
 def solution(mesh):
     in_specs = (
         P("section", "expert", None),
@@ -140,4 +481,6 @@
         P("section", "expert", None, None),
     )
     out_specs = P("section", "expert", None)
+    fused = mesh.shape["expert"] == 4 and mesh.shape["section"] > 2
+    local = local_fused if fused else local_general
     return jax.shard_map(local, mesh=mesh, in_specs=in_specs, out_specs=out_specs, check_vma=False)

time: 200 us -> 103 us (0.52)
  waiting for transfers between devices: 116 us -> 0 us
  Pallas kernels: 0 us -> 95.9 us
  matrix products: 50.6 us -> 0 us
  between operations: 14.1 us -> 0.71 us
  blocking collectives: 5.37 us -> 0 us
  other arithmetic: 7.57 us -> 2.62 us
  starting transfers between devices: 3.09 us -> 0 us
    pallas_call x0 -> x1, Pallas kernels: none -> 95.9 us  [local_fused(): pl.pallas_call(tick_kernel, out_shape=jax.ShapeDtypeStruct(tile, BF16), i...]
    reduce_scatter x2 -> x0, waiting for transfers between devices: 63 us -> none  [the longest x1 31.5 us: local(): lax.psum_scatter(jnp.dot(attended, out_rows, preferred_element_type=jnp.f...]
    dot_general x11 -> x0, matrix products: 45.9 us -> none  [the longest x1 19.9 us: local(): jnp.einsum('ech,ehd->ecd', hidden, expert_out[0], preferred_element_type=...]
    all_gather x2 -> x0, waiting for transfers between devices: 37.4 us -> none  [the longest x1 21 us: local(): gathered = lax.all_gather(normed, 'expert', axis=0, tiled=True)]
    ppermute x1 -> x0, waiting for transfers between devices: 15.2 us -> none  [passed_along(): return lax.ppermute(block, axis, route)]
    all_gather x1 -> x0, blocking collectives: 5.37 us -> none  [local(): routes_all = lax.all_gather(routes, 'expert', axis=0)]
    sub x1 -> x0, matrix products: 4.64 us -> none  [attend_block(): weights = jnp.exp(scores - row_max)]
    transpose x1 -> x0, local copies, waits for them, and re-layouts: 3.23 us -> none  [local(): jnp.einsum('bect,btd->ebcd', slots.astype(jnp.bfloat16), tokens, preferre...]
  transfers between devices with their start and end apart: 5 -> 0, of which waited for: 5 -> 0; matrix products, arithmetic and copies ran while one was open for 0% -> 0% of each run, Pallas kernels for 0% -> 0%
where the time goes in v2:
time: 103 us
  Pallas kernels  95.9 us (93%)
  local copies, waits for them, and re-layouts  3.35 us (3%)
  other arithmetic  2.62 us (3%)
    pallas_call x1, Pallas kernels, local_fused(): pl.pallas_call(tick_kernel, out_shape=jax.ShapeDtypeStruct(tile, BF16), i...  95.9 us

profile of v2, /device:TPU:0, one launch (start us, length us, event | category | flops | bytes accessed | tf_op | source)
XLA Modules:
  0.0 102.6 jit_solution(17273450348214971015)
XLA Ops:
  0.0 0.0 copy-start
  0.7 0.7 fusion.1
  1.4 0.7 compare_bitcast_fusion
  2.0 1.3 %fusion.choice = s32[8,128]{1,0:T(8,128)} fusion(s32[1,128,8]{1,2,0:T(8,128)} %param.14, pred[128]{0:T(512)(128)(4,1)S(1)} %compare_bitcast_fusion), kind=kLoop, calls=%fused_computation.2 | loop fusion | flops 1024 | bytes 8320 | tf_op jit(solution)/shard_map/jit(_where)/select_n | solution.py:412
  3.3 0.8 reshape.27.active
  4.2 0.0 copy-done
  4.2 0.6 dynamic-slice_bitcast_fusion.columns
  4.8 95.9 %shard_map.109 = bf16[4,32,2048]{2,1,0:T(8,128)(2,1)} custom-call(bf16[4,32,2048]{2,1,0:T(8,128)(2,1)} %bitcast.28, s32[8,128]{1,0:T(8,128)} %fusion.choice, s32[4,32,1]{2,1,0:T(8,128)} %reshape.27.active, f32[1,2048]{1,0:T(1,128)} %gain_a.1, f32[1,2048]{1,0:T(1,128)} %gain_e.1, bf16[16,2048]{1,0:T(8,128)(2,1)} %dynamic-slice_bitcast_fusion.columns, ...), custom_call_target="tpu_custom_call" | custom-call | flops 10000000000 | bytes 45000000 | tf_op jit(solution)/shard_map/pallas_call | solution.py:422
  100.7 1.9 %copy.15 = bf16[1,128,2048]{2,1,0:T(8,128)(2,1)} copy(bf16[1,128,2048]{2,1,0:T(8,128)(2,1)} %bitcast.27) | data formatting | bytes 1048576
Async XLA Ops:
  0.0 4.2 %copy-start = (bf16[1,2048,64]{1,2,0:T(8,128)(2,1)S(1)}, bf16[1,2048,64]{1,2,0:T(8,128)(2,1)}, u32[]{:S(2)}) copy-start(bf16[1,2048,64]{1,2,0:T(8,128)(2,1)} %param.19) | copy-start | bytes 786436

commit v3 on v2

--- a/solution.py
+++ b/solution.py
@@ -134,7 +134,7 @@
 
 
 def tick_kernel(
-    carried, choice, active, gain_a, gain_e, columns, w_in, w_out, e_in, e_out, out,
+    carried, routes, halts, lap, active, gain_a, gain_e, router_rows, w_in, w_out, e_in, e_out, out,
     vw_in, vw_out, ve_in, ve_out, packed, incoming, tokens, updated, qkv, heads,
     stage, from_sib, from_cnt, weight, choices,
     load_sem, hop_s, hop_r, gather_s, gather_r, sum_s, sum_r, choice_s, choice_r,
@@ -174,16 +174,16 @@
     ]
     for hop in hops:
         hop.start()
+    choices[me] = jnp.where(halts[...] >= lap[...], routes[...], -1)
     shared = []
     for i, peer in enumerate((sib, cnt, dia)):
         shared.append(
             pltpu.make_async_remote_copy(
-                src_ref=choice, dst_ref=choices.at[me], send_sem=choice_s.at[i],
+                src_ref=choices.at[me], dst_ref=choices.at[me], send_sem=choice_s.at[i],
                 recv_sem=choice_r.at[i], device_id={"expert": peer},
             )
         )
         shared[-1].start()
-    choices[me] = choice[...]
     loads[2].start()
     loads[3].start()
 
@@ -232,7 +232,7 @@
 
     span = 256
 
-    @pl.loop(0, heads.shape[1] // HEAD_SIZE)
+    @pl.loop(0, heads.shape[1] // HEAD_SIZE, unroll=2)
     def _(head):
         cols = pl.ds(pl.multiple_of(lax.rem(head, 2) * HEAD_SIZE, HEAD_SIZE), HEAD_SIZE)
         place = pl.ds(pl.multiple_of(head * HEAD_SIZE, HEAD_SIZE), HEAD_SIZE)
@@ -248,7 +248,7 @@
             col_ids = lax.broadcasted_iota(jnp.int32, scores.shape, 1)
             scores = jnp.where(col_ids <= row_ids, scores, -jnp.inf)
             powers = jnp.exp(scores - jnp.max(scores, axis=-1, keepdims=True))
-            shares = (powers / jnp.sum(powers, axis=-1, keepdims=True)).astype(BF16)
+            shares = (powers * (1.0 / jnp.sum(powers, axis=-1, keepdims=True))).astype(BF16)
             heads[first:upto, place] = jnp.dot(
                 shares, value, preferred_element_type=F32
             ).astype(BF16)
@@ -319,12 +319,14 @@
     for hop in hops:
         hop.wait_send()
 
+    columns = router_rows[pl.ds(pl.multiple_of(me * exp_local, exp_local), exp_local), :]
+
     def dispatch(b):
         names = choices[b]
         own = tokens[b].reshape(block, width)
         gates = jax.nn.sigmoid(
             lax.dot_general(
-                columns[...], own, (((1,), (1,)), ((), ())), preferred_element_type=F32
+                columns, own, (((1,), (1,)), ((), ())), preferred_element_type=F32
             )
         )
         ids = me * exp_local + lax.broadcasted_iota(jnp.int32, (exp_local, block), 0)
@@ -340,10 +342,10 @@
         slot = lax.broadcasted_iota(jnp.int32, (exp_local, SLOT, block), 1).astype(F32)
         match = place[:, None, :] == slot
         chosen = jnp.where(match, 1.0, 0.0).reshape(exp_local * SLOT, block).astype(BF16)
-        scale = jnp.where(match, gates[:, None, :], 0.0).reshape(exp_local * SLOT, block)
+        scale = jnp.where(match, gates[:, None, :], 0.0).reshape(exp_local * SLOT, block).T
         coarse = scale.astype(BF16)
-        weight[b, 0] = coarse
-        weight[b, 1] = (scale - coarse.astype(F32)).astype(BF16)
+        weight[b, :block] = coarse
+        weight[b, block:] = (scale - coarse.astype(F32)).astype(BF16)
 
         @pl.loop(0, width // wide)
         def _(j):
@@ -365,7 +367,7 @@
     loads[2].wait()
     loads[3].wait()
 
-    @pl.loop(0, exp_local)
+    @pl.loop(0, exp_local, unroll=2)
     def _(e):
         arrived = packed[e].reshape(n * SLOT, width)
         hidden = jnp.maximum(jnp.dot(arrived, ve_in[e], preferred_element_type=F32), 0.0)
@@ -376,10 +378,8 @@
 
     def expert_term(number, cols):
         made = packed[:, number, :, cols].reshape(exp_local * SLOT, wide)
-        contract = (((0,), (0,)), ((), ()))
-        return lax.dot_general(
-            weight[number, 0], made, contract, preferred_element_type=F32
-        ) + lax.dot_general(weight[number, 1], made, contract, preferred_element_type=F32)
+        both = jnp.dot(weight[number], made, preferred_element_type=F32)
+        return both[:block] + both[block:]
 
     moves, across, beside = reduce_blocks(
         1, expert_term, (stage.at[1], from_sib.at[1], from_cnt.at[1]),
@@ -409,10 +409,6 @@
     n = lax.axis_size("expert")
     exp_local, _, hid = expert_in.shape[1:]
     active = halting[0] >= section_lap[0]
-    choice = jnp.where(active[None, :], routing[0].T, -1)
-    columns = lax.dynamic_slice_in_dim(
-        router[0].T, lax.axis_index("expert") * exp_local, exp_local, 0
-    )
     weights_in = jnp.transpose(attention_in[0], (1, 0, 2))
     cols = weights_in.shape[2]
     seq = n * tok_dev
@@ -422,7 +418,7 @@
     result = pl.pallas_call(
         tick_kernel,
         out_shape=jax.ShapeDtypeStruct(tile, BF16),
-        in_specs=[far] + [vmem] * 5 + [far] * 4,
+        in_specs=[far] + [vmem] * 7 + [far] * 4,
         out_specs=vmem,
         scratch_shapes=[
             pltpu.VMEM(weights_in.shape, BF16),
@@ -438,8 +434,8 @@
             pltpu.VMEM((2,) + tile, BF16),
             pltpu.VMEM((2,) + tile, BF16),
             pltpu.VMEM((2,) + tile, BF16),
-            pltpu.VMEM((n, 2, exp_local * SLOT, tok_dev), BF16),
-            pltpu.VMEM((n,) + choice.shape, jnp.int32),
+            pltpu.VMEM((n, 2 * tok_dev, exp_local * SLOT), BF16),
+            pltpu.VMEM((n, routing.shape[2], tok_dev), jnp.int32),
             dma((4,)), dma((CHUNKS,)), dma((CHUNKS,)),
             dma((2, 3, CHUNKS)), dma((2, 3, CHUNKS)),
             dma((2, 3, CHUNKS)), dma((2, 3, CHUNKS)),
@@ -453,11 +449,13 @@
         ),
     )(
         carried[0].reshape(tile),
-        choice,
+        routing[0].T,
+        halting,
+        section_lap.reshape(1, 1),
         active.astype(jnp.int32).reshape(CHUNKS, rows, 1),
         attention_gain,
         expert_gain,
-        columns,
+        router[0].T,
         weights_in,
         attention_out[0],
         expert_in[0],

time: 103 us -> 96.1 us (0.933)
  Pallas kernels: 95.9 us -> 91.8 us
  other arithmetic: 2.62 us -> 0.67 us
    pallas_call x1, Pallas kernels: 95.9 us -> 91.8 us  [local_fused(): pl.pallas_call(tick_kernel, out_shape=jax.ShapeDtypeStruct(tile, BF16), i...]
    select_n x1 -> x0, other arithmetic: 1.28 us -> none  [local_fused(): choice = jnp.where(active[None, :], routing[0].T, -1)]
where the time goes in v3:
time: 96.1 us; the launch traced here: 95.9 us
  Pallas kernels  91.8 us (96%)
  local copies, waits for them, and re-layouts  2.72 us (3%)
    pallas_call x1, Pallas kernels, local_fused(): pl.pallas_call(tick_kernel, out_shape=jax.ShapeDtypeStruct(tile, BF16), i...  91.8 us

profile of v3, /device:TPU:0, one launch (start us, length us, event | category | flops | bytes accessed | tf_op | source)
XLA Modules:
  0.0 95.9 jit_solution(6431635264395878365)
XLA Ops:
  0.7 0.7 fusion
  1.3 0.8 reshape.27.active
  2.2 91.8 %shard_map.109 = bf16[4,32,2048]{2,1,0:T(8,128)(2,1)} custom-call(bf16[4,32,2048]{2,1,0:T(8,128)(2,1)} %bitcast.23, s32[8,128]{1,0:T(8,128)} %bitcast.25, s32[1,128]{1,0:T(1,128)} %halts.1, s32[1,1]{1,0:T(1,128)} %bitcast.16.lap, s32[4,32,1]{2,1,0:T(8,128)} %reshape.27.active, f32[1,2048]{1,0:T(1,128)} %gain_a.1, f32[1,2048]{1,0:T(1,128)} %gain_e.1, ...), custom_call_target="tpu_custom_call" | custom-call | flops 10000000000 | bytes 45000000 | tf_op jit(solution)/shard_map/pallas_call | solution.py:418
  94.0 1.9 %copy.15 = bf16[1,128,2048]{2,1,0:T(8,128)(2,1)} copy(bf16[1,128,2048]{2,1,0:T(8,128)(2,1)} %bitcast.21) | data formatting | bytes 1048576
